TPU v7x, 128 devices: a whole 4x4x4 slice. The times are simulated.
128 devices in a mesh: wide: 64 (over z, x, y_hi, core), narrow: 2 (over y_lo).
Axes of the slice: x: 4, y: 4 (y_hi: 2, y_lo: 2; y = y_hi * 2 + y_lo), z: 4, core: 2. Of those that a mesh axis runs over, the one named last changes fastest.
Arguments:
- coeffs: float32 [7680, 7680], P('narrow', 'wide'), may hold values from -6 to 6
- diagonal: float32 [7680, 7680], P('narrow', 'wide'), may hold values from 0.5 to 3
- tile_cols: int32 [60, 20], P('narrow'), may hold values from 0 to 59, as said below
- tile_vals: bfloat16 [60, 20, 128, 128], P('narrow'), may hold values from -3 to 3, as said below
Outputs:
- sigma: float32 [7680, 7680], P('narrow', 'wide')
Inputs may be any that keep to these rules, and one draw needn't show every extreme that they name: `tile_cols`: row I lists 20 different tile columns, never I itself; J is listed in row I exactly when I is listed in row J. Where tile_cols[I, k] = J and tile_cols[J, m] = I, tile_vals[J, m] is the transpose of tile_vals[I, k], so H is symmetric.
All inputs are finite; a program needn't handle non-finite values.
Results may differ from a plain program's by a relative error of at most 0.0023.
Values may be sent and summed in bfloat16 or wider, within the bound.
A program may use at most 192 MiB of HBM per device.

v0:
```python
import math

import jax
import jax.numpy as jnp
from jax import lax
from jax.sharding import PartitionSpec as P


def rows_apply(gathered, tile_cols, tile_vals):
    tile_size = tile_vals.shape[-1]
    blocks = gathered.reshape(gathered.shape[0] // tile_size, tile_size, gathered.shape[1])
    picked = blocks[tile_cols]
    result = jnp.einsum("ikab,ikbm->iam", tile_vals, picked, preferred_element_type=jnp.float32)
    return result.reshape(-1, gathered.shape[1])


def cols_apply(gathered, tile_cols, tile_vals):
    tile_size = tile_vals.shape[-1]
    blocks = gathered.reshape(gathered.shape[0], gathered.shape[1] // tile_size, tile_size)
    picked = blocks[:, tile_cols]
    result = jnp.einsum("aikb,ikcb->aic", picked, tile_vals, preferred_element_type=jnp.float32)
    return result.reshape(gathered.shape[0], -1)


def per_device(coeffs, diagonal, tile_cols, tile_vals):
    tile_size = tile_vals.shape[-1]
    degree = tile_vals.shape[1]
    weight_scale = 1.0 / math.sqrt(degree * tile_size)
    coeff_low = coeffs.astype(jnp.bfloat16)
    gathered = lax.all_gather(coeff_low, "narrow", axis=0, tiled=True)
    sigma_alpha = rows_apply(gathered, tile_cols, tile_vals)
    moved = lax.all_to_all(
        lax.all_to_all(coeff_low, "wide", split_axis=0, concat_axis=1, tiled=True),
        "narrow",
        split_axis=1,
        concat_axis=0,
        tiled=True,
    )
    widened = lax.all_gather(moved, "narrow", axis=1, tiled=True)
    sigma_beta = cols_apply(widened, tile_cols, tile_vals)
    returned = lax.all_to_all(
        lax.all_to_all(sigma_beta, "narrow", split_axis=0, concat_axis=1, tiled=True),
        "wide",
        split_axis=1,
        concat_axis=0,
        tiled=True,
    )
    return weight_scale * sigma_alpha + weight_scale * returned + diagonal * coeffs


def solution(mesh):
    in_specs = (
        P("narrow", "wide"),
        P("narrow", "wide"),
        P("narrow", None),
        P("narrow", None, None, None),
    )
    out_specs = P("narrow", "wide")
    return jax.shard_map(
        per_device, mesh=mesh, in_specs=in_specs, out_specs=out_specs, check_vma=False
    )
```

profile of v0, /device:TPU:1, one launch (start us, length us, event | category | flops | bytes accessed | tf_op | source)
XLA Modules:
  0.0 225.4 jit_solution(1890006085144712298)
XLA Ops:
  6.5 0.0 all-gather.5.cloned.1.call-start
  6.5 1.6 convert_element_type.3
  8.1 0.0 copy-start
  8.1 1.3 copy.20
  9.4 1.5 all_to_all.48
  10.9 0.0 copy-done
  10.9 31.8 %all_to_all.64 = bf16[64,60,120]{2,1,0:T(8,128)(2,1)S(1)} all-to-all(bf16[64,60,120]{2,1,0:T(8,128)(2,1)S(1)} %all_to_all.48), channel_id=1, replica_groups=mesh['wide'=64,'narrow'=2] {'wide'}, dimensions={0} | all-to-all | bytes 1843200 | tf_op jit(solution)/shard_map/all_to_all | solution.py:33
  42.7 0.6 copy.21
  43.4 2.1 all_to_all.51
  45.5 0.1 copy.22
  45.6 14.9 %all_to_all.65 = bf16[60,2,3840]{2,0,1:T(8,128)(2,1)S(1)} all-to-all(bf16[60,2,3840]{2,0,1:T(8,128)(2,1)S(1)} %copy.22), channel_id=1, replica_groups=mesh['wide'=64,'narrow'=2] {'narrow'}, dimensions={1} | all-to-all | bytes 1843200 | tf_op jit(solution)/shard_map/all_to_all | solution.py:32
  60.5 0.0 copy-start.1
  60.5 1.1 all_to_all.54
  61.7 0.0 all-gather.5.cloned.1.call-update
  61.7 0.0 all-gather.3.cloned.1.call-start
  61.7 0.7 all-gather.3.cloned.1.call-update
  62.4 0.0 copy-done.1
  62.5 0.1 copy.17
  62.6 0.1 reshape.31
  62.7 28.1 %all-gather.5.cloned.1.call-done = bf16[120,7680]{1,0:T(8,128)(2,1)} async-done(((bf16[120,3840]{1,0:T(8,128)(2,1)}), bf16[120,7680]{1,0:T(8,128)(2,1)}) %all-gather.5.cloned.1.call-update) | async-done | bytes 1843216 | tf_op jit(solution)/shard_map/all_gather | solution.py:39
  90.8 1.8 copy_bitcast_fusion
  92.6 16.6 %gather_fusion.1 = bf16[600,120,128]{2,1,0:T(8,128)(2,1)} fusion(bf16[120,60,128]{2,0,1:T(8,128)(2,1)S(1)} %copy_bitcast_fusion, s32[1024]{0:T(1024)S(1)} %pad_clamp_fusion), kind=kCustom, calls=%fused_computation.1 | custom fusion | bytes 36866400 | tf_op jit(solution)/shard_map/gather | solution.py:20
  109.2 15.9 %convolution_bitcast_fusion = f32[120,30,128]{2,0,1:T(8,128)} fusion(bf16[120,30,20,128]{3,0,2,1:T(8,128)(2,1)} %bitcast.40, bf16[30,20,128,128]{3,2,1,0:T(8,128)(2,1)} %param.7), kind=kOutput, calls=%fused_computation.9 | convolution fusion | flops 2359296000 | bytes 39936000 | tf_op jit(solution)/shard_map/aikb,ikcb->aic/dot_general | solution.py:21
  125.1 1.9 copy.24
  127.0 1.6 all_to_all.55
  128.7 5.0 %all-to-all-start.2 = ((f32[2,60,3840]{2,1,0:T(8,128)}), f32[2,60,3840]{2,1,0:T(8,128)}, u32[]{:S(2)}, u32[]{:S(2)}) async-start(f32[2,60,3840]{2,1,0:T(8,128)} %all_to_all.55), calls=%async_computation.2 | async-start | bytes 3932160 | tf_op jit(solution)/shard_map/all_to_all | solution.py:42
  133.6 0.0 all-gather.3.cloned.1.call-done
  133.6 1.8 copy_bitcast_fusion.1
  135.5 16.7 %gather_fusion = bf16[600,128,120]{1,2,0:T(8,128)(2,1)} fusion(bf16[60,128,120]{1,2,0:T(8,128)(2,1)S(1)} %copy_bitcast_fusion.1, s32[1024]{0:T(1024)S(1)} %pad_clamp_fusion), kind=kCustom, calls=%fused_computation | custom fusion | bytes 36866400 | tf_op jit(solution)/shard_map/gather | solution.py:12
  152.1 4.2 %all-to-all-done.2 = f32[2,60,3840]{2,1,0:T(8,128)} async-done(((f32[2,60,3840]{2,1,0:T(8,128)}), f32[2,60,3840]{2,1,0:T(8,128)}, u32[]{:S(2)}, u32[]{:S(2)}) %all-to-all-start.2) | async-done | bytes 1843232 | tf_op jit(solution)/shard_map/all_to_all | solution.py:42
  156.4 4.2 %copy.25 = f32[60,2,3840]{2,1,0:T(2,128)} copy(f32[60,2,3840]{2,0,1:T(8,128)} %bitcast.11) | data formatting | bytes 3686400 | tf_op jit(solution)/shard_map/all_to_all | solution.py:42
  160.6 4.2 %all_to_all.58 = f32[60,64,120]{2,1,0:T(8,128)S(1)} reshape(f32[60,2,3840]{2,1,0:T(2,128)} %copy.25) | data formatting | bytes 3686400 | tf_op jit(solution)/shard_map/all_to_all | solution.py:41
  164.7 2.5 %copy.26 = f32[60,64,120]{2,0,1:T(8,128)} copy(f32[60,64,120]{2,1,0:T(8,128)S(1)} %all_to_all.58) | data formatting | bytes 3686400 | tf_op jit(solution)/shard_map/all_to_all | solution.py:41
  167.2 11.1 %all-to-all-start.3 = ((f32[60,64,120]{2,0,1:T(8,128)}), f32[60,64,120]{2,0,1:T(8,128)S(1)}, u32[]{:S(2)}, u32[]{:S(2)}) async-start(f32[60,64,120]{2,0,1:T(8,128)} %copy.26), calls=%async_computation.3 | async-start | bytes 4194304 | tf_op jit(solution)/shard_map/all_to_all | solution.py:41
  178.3 16.1 %fusion.1 = f32[30,15,8,128]{3,2,1,0:T(8,128)} fusion(bf16[30,20,128,120]{2,3,1,0:T(8,128)(2,1)} %bitcast.41, bf16[30,20,128,128]{3,2,1,0:T(8,128)(2,1)} %param.7), kind=kOutput, calls=%fused_computation.8 | convolution fusion | flops 2359756800 | bytes 39936000 | tf_op jit(solution)/shard_map/ikab,ikbm->iam/dot_general | solution.py:13
  194.4 14.4 %all-to-all-done.3 = f32[60,64,120]{2,0,1:T(8,128)S(1)} async-done(((f32[60,64,120]{2,0,1:T(8,128)}), f32[60,64,120]{2,0,1:T(8,128)S(1)}, u32[]{:S(2)}, u32[]{:S(2)}) %all-to-all-start.3) | async-done | bytes 1843232 | tf_op jit(solution)/shard_map/all_to_all | solution.py:41
  208.8 1.5 multiply_bitcast_fusion
  210.4 1.6 mul.26
  212.0 1.8 copy.27
  213.7 4.8 %fusion = f32[3840,120]{0,1:T(8,128)} fusion(f32[3840,120]{0,1:T(8,128)} %copy.27, f32[30,15,8,128]{3,2,1,0:T(8,128)} %fusion.1, f32[3840,120]{0,1:T(8,128)} %param.5, f32[3840,120]{0,1:T(8,128)} %param.4), kind=kLoop, calls=%fused_computation.4 | loop fusion | flops 1382400 | bytes 9216000 | tf_op jit(solution)/shard_map/add | solution.py:48
  (2 shorter events, 0.0 us)
Async XLA Ops:
  6.5 84.3 %all-gather.5.cloned.1.call-start = ((), (), s32[]{:S(2)}) async-start(), calls=%async_computation.5 | async-start | bytes 2764800 | tf_op jit(solution)/shard_map/all_gather | solution.py:39
  8.1 2.8 %copy-start = (bf16[3840,120]{0,1:T(8,128)(2,1)}, bf16[3840,120]{0,1:T(8,128)(2,1)S(1)}, u32[]{:S(2)}) copy-start(bf16[3840,120]{0,1:T(8,128)(2,1)S(1)} %convert_element_type.3) | copy-start | bytes 2764804
  60.5 1.9 copy-start.1
  61.7 72.0 %all-gather.3.cloned.1.call-start = ((), (), s32[]{:S(2)}) async-start(), calls=%async_computation.4 | async-start | bytes 2764800 | tf_op jit(solution)/shard_map/all_gather | solution.py:30
  128.7 27.7 %all-to-all-start.2 = ((f32[2,60,3840]{2,1,0:T(8,128)}), f32[2,60,3840]{2,1,0:T(8,128)}, u32[]{:S(2)}, u32[]{:S(2)}) async-start(f32[2,60,3840]{2,1,0:T(8,128)} %all_to_all.55), calls=%async_computation.2 | async-start | bytes 3932160 | tf_op jit(solution)/shard_map/all_to_all | solution.py:42
  167.2 41.6 %all-to-all-start.3 = ((f32[60,64,120]{2,0,1:T(8,128)}), f32[60,64,120]{2,0,1:T(8,128)S(1)}, u32[]{:S(2)}, u32[]{:S(2)}) async-start(f32[60,64,120]{2,0,1:T(8,128)} %copy.26), calls=%async_computation.3 | async-start | bytes 4194304 | tf_op jit(solution)/shard_map/all_to_all | solution.py:41
Sparse Core Ops, SparseCore 0:
  61.8 28.9 all-gather.4
  92.5 33.7 all-gather.2
where the time goes:
time: 226 us; the launch traced here: 225 us
  local copies, waits for them, and re-layouts  61.6 us (27%)
  waiting for transfers between devices  47.5 us (21%)
  blocking collectives  46.7 us (21%)
  matrix products  32 us (14%)
  starting transfers between devices  16.1 us (7%)
  between operations  13.5 us (6%)
  other arithmetic  7.97 us (4%)
    all_to_all x1, blocking collectives, per_device(): lax.all_to_all(coeff_low, 'wide', split_axis=0, concat_axis=1, tiled=True)  31.8 us
    all_gather x1, waiting for transfers between devices, per_device(): widened = lax.all_gather(moved, 'narrow', axis=1, tiled=True)  28.1 us
    gather x1, local copies, waits for them, and re-layouts, rows_apply(): picked = blocks[tile_cols]  16.7 us
    gather x1, local copies, waits for them, and re-layouts, cols_apply(): picked = blocks[:, tile_cols]  16.6 us
    dot_general x1, matrix products, rows_apply(): jnp.einsum('ikab,ikbm->iam', tile_vals, picked, preferred_element_type=jn...  16.1 us
    dot_general x1, matrix products, cols_apply(): jnp.einsum('aikb,ikcb->aic', picked, tile_vals, preferred_element_type=jn...  15.9 us
    all_to_all x1, blocking collectives, per_device(): lax.all_to_all(lax.all_to_all(coeff_low, 'wide', split_axis=0, concat_axi...  14.9 us
    all_to_all x1, waiting for transfers between devices, per_device(): lax.all_to_all(lax.all_to_all(sigma_beta, 'narrow', split_axis=0, concat_...  14.4 us
  transfers between devices with their start and end apart: 4, of which 3 were waited for; matrix products, arithmetic and copies ran while one was open for 32% of the time, Pallas kernels for 0%

commit v1 on v0

v1 whole, which is shorter than its diff:
```python
import functools
import math

import jax
import jax.numpy as jnp
from jax import lax
from jax.experimental import pallas as pl
from jax.experimental.pallas import tpu as pltpu
from jax.sharding import PartitionSpec as P

MESH = pl.DeviceIdType.MESH
TILE = 128
PER_PLANE = 16
TILES_PER_PLANE = 15


def kernel(
    cols_ref,
    coeff_hbm,
    diag_hbm,
    vals_hbm,
    out_ref,
    coeff_v,
    diag_v,
    vals_v,
    x_ref,
    y_ref,
    yt_ref,
    acc_ref,
    alpha_ref,
    send_ref,
    back_ref,
    local_sem,
    pair_send,
    pair_recv,
    fwd_send,
    fwd_recv,
    ret_send,
    ret_recv,
    *,
    wide,
    scale,
):
    w = lax.axis_index("wide")
    n = lax.axis_index("narrow")
    other = 1 - n
    half = out_ref.shape[1] // TILE
    width = out_ref.shape[0]
    degree = cols_ref.shape[1]
    half_wide = wide // 2

    coeff_copy = pltpu.make_async_copy(coeff_hbm, coeff_v, local_sem.at[0])
    coeff_copy.start()
    vals_copy = pltpu.make_async_copy(vals_hbm, vals_v, local_sem.at[1])
    vals_copy.start()
    diag_copy = pltpu.make_async_copy(diag_hbm, diag_v, local_sem.at[2])
    diag_copy.start()
    coeff_copy.wait()

    for i in range(half):
        x_ref[n * half + i] = coeff_v[:, i * TILE : (i + 1) * TILE].astype(jnp.bfloat16)

    own_half = x_ref.at[pl.ds(n * half, half)]
    pair = pltpu.make_async_remote_copy(
        src_ref=own_half,
        dst_ref=own_half,
        send_sem=pair_send,
        recv_sem=pair_recv,
        device_id=(w, other),
        device_id_type=MESH,
    )
    pair.start()

    def send_forward(step, carry):
        i = lax.rem(w + step, half)
        tile = n * half + i
        to = tile + tile // TILES_PER_PLANE
        for to_n in (0, 1):
            mine = jnp.logical_and(to == w, n == to_n)

            @pl.when(mine)
            def _():
                pltpu.make_async_copy(x_ref.at[tile], y_ref.at[w], fwd_recv).start()

            @pl.when(jnp.logical_not(mine))
            def _():
                pltpu.make_async_remote_copy(
                    src_ref=x_ref.at[tile],
                    dst_ref=y_ref.at[w],
                    send_sem=fwd_send,
                    recv_sem=fwd_recv,
                    device_id=(to, to_n),
                    device_id_type=MESH,
                ).start()

        return carry

    lax.fori_loop(0, half, send_forward, 0)

    group = w // PER_PLANE
    place = lax.rem(w, PER_PLANE)
    active = place < TILES_PER_PLANE
    my_tile = group * TILES_PER_PLANE + place
    tile_half = my_tile // half
    slot = lax.rem(my_tile, half)

    vals_copy.wait()
    pair.wait_recv()

    def alpha_step(row, carry):
        lhs = jnp.concatenate([x_ref[cols_ref[row, k]] for k in range(degree)], axis=1)
        rhs = jnp.concatenate([vals_v[row, k] for k in range(degree)], axis=1)
        alpha_ref[row] = lax.dot_general(
            lhs, rhs, (((1,), (1,)), ((), ())), preferred_element_type=jnp.float32
        )
        return carry

    lax.fori_loop(0, half, alpha_step, 0)

    @pl.when(active)
    def _():
        pltpu.make_async_copy(y_ref, y_ref, fwd_recv).wait()

        def repack(g, carry):
            for t in range(TILES_PER_PLANE):
                low, high = t * TILE, (t + 1) * TILE
                pieces = []
                while low < high:
                    source, begin = low // width, low % width
                    end = min(width, begin + high - low)
                    piece = y_ref[g * PER_PLANE + source].astype(jnp.float32)
                    pieces.append(piece[begin:end])
                    low += end - begin
                yt_ref[g * TILES_PER_PLANE + t] = jnp.concatenate(pieces, axis=0).astype(
                    jnp.bfloat16
                )
            return carry

        lax.fori_loop(0, wide // PER_PLANE, repack, 0)

        def send_chunk(j):
            send_ref[j] = acc_ref[pl.ds(pl.multiple_of(j * width, 8), width), :].astype(
                jnp.bfloat16
            )
            to = n * half_wide + j
            mine = jnp.logical_and(to == w, tile_half == n)

            @pl.when(mine)
            def _():
                pltpu.make_async_copy(send_ref.at[j], back_ref.at[slot], ret_recv).start()

            @pl.when(jnp.logical_not(mine))
            def _():
                pltpu.make_async_remote_copy(
                    src_ref=send_ref.at[j],
                    dst_ref=back_ref.at[slot],
                    send_sem=ret_send,
                    recv_sem=ret_recv,
                    device_id=(to, tile_half),
                    device_id_type=MESH,
                ).start()

        def chunk_of(row):
            return row + row // TILES_PER_PLANE

        first = lax.rem(w * 7, half)

        def beta_step(step, carry):
            row = lax.rem(first + step, half)
            lhs = jnp.concatenate([vals_v[row, k] for k in range(degree)], axis=1)
            rhs = jnp.concatenate(
                [yt_ref[cols_ref[row, k]] for k in range(degree)],
                axis=0,
            )
            acc_ref[pl.ds(pl.multiple_of(row * TILE, TILE), TILE), :] = jnp.dot(
                lhs, rhs, preferred_element_type=jnp.float32
            )

            @pl.when(step > 0)
            def _():
                send_chunk(chunk_of(row))

            @pl.when(lax.rem(row, TILES_PER_PLANE) == TILES_PER_PLANE - 1)
            def _():
                send_chunk(chunk_of(row) + 1)

            return carry

        lax.fori_loop(0, half, beta_step, 0)
        send_chunk(chunk_of(first))

    diag_copy.wait()
    pltpu.make_async_copy(back_ref, back_ref, ret_recv).wait()

    for i in range(half):
        part = slice(i * TILE, (i + 1) * TILE)
        out_ref[:, part] = (
            scale * alpha_ref[i]
            + scale * back_ref[i].astype(jnp.float32)
            + diag_v[:, part] * coeff_v[:, part]
        )

    pair.wait_send()
    has_own = jnp.logical_and(active, tile_half == n)

    @pl.when(has_own)
    def _():
        pltpu.make_async_copy(
            x_ref.at[pl.ds(0, 2 * half - 1)], x_ref.at[pl.ds(0, 2 * half - 1)], fwd_send
        ).wait()

    @pl.when(jnp.logical_not(has_own))
    def _():
        pltpu.make_async_copy(x_ref, x_ref, fwd_send).wait()

    own_return = jnp.logical_and(has_own, w // half_wide == n)

    @pl.when(jnp.logical_and(active, own_return))
    def _():
        done = send_ref.at[pl.ds(0, half_wide - 1)]
        pltpu.make_async_copy(done, done, ret_send).wait()

    @pl.when(jnp.logical_and(active, jnp.logical_not(own_return)))
    def _():
        pltpu.make_async_copy(send_ref, send_ref, ret_send).wait()


def solution(mesh):
    wide = mesh.shape["wide"]

    def per_device(coeffs, diagonal, tile_cols, tile_vals):
        rows, width = coeffs.shape
        half, degree = tile_cols.shape
        scale = 1.0 / math.sqrt(degree * TILE)
        any_space = pl.BlockSpec(memory_space=pl.ANY)
        out = pl.pallas_call(
            functools.partial(kernel, wide=wide, scale=scale),
            out_shape=jax.ShapeDtypeStruct((width, rows), jnp.float32),
            in_specs=[
                pl.BlockSpec(memory_space=pltpu.SMEM),
                any_space,
                any_space,
                any_space,
            ],
            out_specs=pl.BlockSpec(memory_space=pltpu.VMEM),
            scratch_shapes=[
                pltpu.VMEM((width, rows), jnp.float32),
                pltpu.VMEM((width, rows), jnp.float32),
                pltpu.VMEM((half, degree, TILE, TILE), jnp.bfloat16),
                pltpu.VMEM((2 * half, width, TILE), jnp.bfloat16),
                pltpu.VMEM((wide, width, TILE), jnp.bfloat16),
                pltpu.VMEM((2 * half, TILE, TILE), jnp.bfloat16),
                pltpu.VMEM((rows, TILE), jnp.float32),
                pltpu.VMEM((half, width, TILE), jnp.float32),
                pltpu.VMEM((wide // 2, width, TILE), jnp.bfloat16),
                pltpu.VMEM((half, width, TILE), jnp.bfloat16),
                pltpu.SemaphoreType.DMA((3,)),
                pltpu.SemaphoreType.DMA,
                pltpu.SemaphoreType.DMA,
                pltpu.SemaphoreType.DMA,
                pltpu.SemaphoreType.DMA,
                pltpu.SemaphoreType.DMA,
                pltpu.SemaphoreType.DMA,
            ],
            compiler_params=pltpu.CompilerParams(
                has_side_effects=True, vmem_limit_bytes=52 * 1024 * 1024
            ),
        )(tile_cols, coeffs.T, diagonal.T, tile_vals)
        return out.T

    in_specs = (
        P("narrow", "wide"),
        P("narrow", "wide"),
        P("narrow", None),
        P("narrow", None, None, None),
    )
    return jax.shard_map(
        per_device,
        mesh=mesh,
        in_specs=in_specs,
        out_specs=P("narrow", "wide"),
        check_vma=False,
    )
```

time: 226 us -> 90.1 us (0.40)
  Pallas kernels: 0 us -> 86.7 us
  local copies, waits for them, and re-layouts: 61.6 us -> 2.03 us
  waiting for transfers between devices: 47.5 us -> 0 us
  blocking collectives: 46.7 us -> 0 us
  matrix products: 32 us -> 0 us
  starting transfers between devices: 16.1 us -> 0 us
  between operations: 13.5 us -> 0.01 us
  other arithmetic: 7.97 us -> 0 us
    pallas_call x0 -> x1, Pallas kernels: none -> 86.7 us  [per_device(): pl.pallas_call(functools.partial(kernel, wide=wide, scale=scale), out_sha...]
    all_to_all x2 -> x0, blocking collectives: 46.7 us -> none  [the longest x1 31.8 us: per_device(): lax.all_to_all(coeff_low, 'wide', split_axis=0, concat_axis=1, tiled=True)]
    gather x2 -> x0, local copies, waits for them, and re-layouts: 33.2 us -> none  [the longest x1 16.7 us: rows_apply(): picked = blocks[tile_cols]]
    dot_general x2 -> x0, matrix products: 32 us -> none  [the longest x1 16.1 us: rows_apply(): jnp.einsum('ikab,ikbm->iam', tile_vals, picked, preferred_element_type=jn...]
    all_gather x2 -> x0, waiting for transfers between devices: 28.2 us -> none  [the longest x1 28.1 us: per_device(): widened = lax.all_gather(moved, 'narrow', axis=1, tiled=True)]
    all_to_all x2 -> x0, waiting for transfers between devices: 18.6 us -> none  [the longest x1 14.4 us: per_device(): lax.all_to_all(lax.all_to_all(sigma_beta, 'narrow', split_axis=0, concat_...]
    all_to_all x9 -> x0, local copies, waits for them, and re-layouts: 17.9 us -> none  [the longest x2 6.65 us: per_device(): lax.all_to_all(lax.all_to_all(sigma_beta, 'narrow', split_axis=0, concat_...]
    all_to_all x2 -> x0, starting transfers between devices: 16.1 us -> none  [the longest x1 11.1 us: per_device(): lax.all_to_all(lax.all_to_all(sigma_beta, 'narrow', split_axis=0, concat_...]
  transfers between devices with their start and end apart: 4 -> 0, of which waited for: 3 -> 0; matrix products, arithmetic and copies ran while one was open for 32% -> 0% of each run, Pallas kernels for 0% -> 0%
where the time goes in v1:
time: 90.1 us; the launch traced here: 88.7 us
  Pallas kernels  86.7 us (96%)
  local copies, waits for them, and re-layouts  2.03 us (2%)
    pallas_call x1, Pallas kernels, per_device(): pl.pallas_call(functools.partial(kernel, wide=wide, scale=scale), out_sha...  86.7 us
    unnamed x2, local copies, waits for them, and re-layouts  2.03 us

profile of v1, /device:TPU:1, one launch (start us, length us, event | category | flops | bytes accessed | tf_op | source)
XLA Modules:
  0.0 88.7 jit_solution(8430472885586439305)
XLA Ops:
  0.0 0.8 copy.5.cols_ref
  0.8 86.7 %shard_map.46 = f32[120,3840]{1,0:T(8,128)S(1)} custom-call(s32[30,20]{1,0:T(8,128)S(1)} %copy.5.cols_ref, f32[120,3840]{1,0:T(8,128)} %bitcast.4, f32[120,3840]{1,0:T(8,128)} %bitcast.5, bf16[30,20,128,128]{3,2,1,0:T(8,128)(2,1)} %vals_hbm.1), custom_call_target="tpu_custom_call" | custom-call | tf_op jit(solution)/shard_map/pallas_call | solution.py:236
  87.5 1.2 %copy.7 = f32[3840,120]{0,1:T(8,128)} copy(f32[3840,120]{0,1:T(8,128)S(1)} %bitcast.3) | data formatting | bytes 3686400

commit v2 on v1

--- a/solution.py
+++ b/solution.py
@@ -10,8 +10,10 @@
 
 MESH = pl.DeviceIdType.MESH
 TILE = 128
-PER_PLANE = 16
-TILES_PER_PLANE = 15
+PIECES = 5
+PER_SIDE = 16
+GROUP_SLICES = 16
+GROUP_TILES = 15
 
 
 def kernel(
@@ -46,7 +48,7 @@
     other = 1 - n
     half = out_ref.shape[1] // TILE
     width = out_ref.shape[0]
-    degree = cols_ref.shape[1]
+    degree = cols_ref.shape[0]
     half_wide = wide // 2
 
     coeff_copy = pltpu.make_async_copy(coeff_hbm, coeff_v, local_sem.at[0])
@@ -55,88 +57,111 @@
     vals_copy.start()
     diag_copy = pltpu.make_async_copy(diag_hbm, diag_v, local_sem.at[2])
     diag_copy.start()
+
+    barrier = pltpu.get_barrier_semaphore()
+
+    def greet(step, carry):
+        to = lax.rem(w + step, wide)
+
+        @pl.when(step > 0)
+        def _():
+            pl.semaphore_signal(barrier, inc=1, device_id=(to, n), device_id_type=MESH)
+
+        pl.semaphore_signal(barrier, inc=1, device_id=(to, other), device_id_type=MESH)
+        return carry
+
+    lax.fori_loop(0, wide, greet, 0)
     coeff_copy.wait()
 
     for i in range(half):
         x_ref[n * half + i] = coeff_v[:, i * TILE : (i + 1) * TILE].astype(jnp.bfloat16)
 
-    own_half = x_ref.at[pl.ds(n * half, half)]
-    pair = pltpu.make_async_remote_copy(
-        src_ref=own_half,
-        dst_ref=own_half,
-        send_sem=pair_send,
-        recv_sem=pair_recv,
-        device_id=(w, other),
-        device_id_type=MESH,
-    )
-    pair.start()
-
-    def send_forward(step, carry):
-        i = lax.rem(w + step, half)
-        tile = n * half + i
-        to = tile + tile // TILES_PER_PLANE
-        for to_n in (0, 1):
-            mine = jnp.logical_and(to == w, n == to_n)
-
-            @pl.when(mine)
-            def _():
-                pltpu.make_async_copy(x_ref.at[tile], y_ref.at[w], fwd_recv).start()
-
-            @pl.when(jnp.logical_not(mine))
-            def _():
-                pltpu.make_async_remote_copy(
-                    src_ref=x_ref.at[tile],
-                    dst_ref=y_ref.at[w],
-                    send_sem=fwd_send,
-                    recv_sem=fwd_recv,
-                    device_id=(to, to_n),
-                    device_id_type=MESH,
-                ).start()
-
+    pl.semaphore_wait(barrier, 2 * wide - 1)
+
+    piece = half // PIECES
+    pair = []
+    for j in range(PIECES):
+        part = x_ref.at[pl.ds(n * half + j * piece, piece)]
+        copy = pltpu.make_async_remote_copy(
+            src_ref=part,
+            dst_ref=part,
+            send_sem=pair_send.at[j],
+            recv_sem=pair_recv.at[j],
+            device_id=(w, other),
+            device_id_type=MESH,
+        )
+        copy.start()
+        pair.append(copy)
+
+    my_plane = lax.rem(w // 2, 2)
+
+    def send_forward(tile):
+        side, rank = tile // half, lax.rem(tile, half)
+        plane = lax.rem(rank, 2)
+        spot = side * (PER_SIDE - 1) + rank // 2
+        spot = spot + spot // (PER_SIDE - 1)
+        to = (spot // 2) * 4 + plane * 2 + lax.rem(spot, 2)
+        to_n = jnp.where(plane == my_plane, n, other)
+        mine = jnp.logical_and(to == w, to_n == n)
+
+        @pl.when(mine)
+        def _():
+            pltpu.make_async_copy(x_ref.at[tile], y_ref.at[w], fwd_recv).start()
+
+        @pl.when(jnp.logical_not(mine))
+        def _():
+            pltpu.make_async_remote_copy(
+                src_ref=x_ref.at[tile],
+                dst_ref=y_ref.at[w],
+                send_sem=fwd_send,
+                recv_sem=fwd_recv,
+                device_id=(to, to_n),
+                device_id_type=MESH,
+            ).start()
+
+    def send_own(step, carry):
+        send_forward(n * half + lax.rem(w * 7 + step, half))
         return carry
 
-    lax.fori_loop(0, half, send_forward, 0)
-
-    group = w // PER_PLANE
-    place = lax.rem(w, PER_PLANE)
-    active = place < TILES_PER_PLANE
-    my_tile = group * TILES_PER_PLANE + place
-    tile_half = my_tile // half
-    slot = lax.rem(my_tile, half)
+    lax.fori_loop(0, half, send_own, 0)
+
+    for j in range(PIECES):
+        pair[j].wait_recv()
+
+        def send_relayed(step, carry):
+            send_forward(other * half + j * piece + lax.rem(w + step, piece))
+            return carry
+
+        lax.fori_loop(0, piece, send_relayed, 0)
+
+    my_spot = (w // 4) * 2 + lax.rem(w, 2)
+    tile_half = my_spot // PER_SIDE
+    place = lax.rem(my_spot, PER_SIDE)
+    active = place < PER_SIDE - 1
+    slot = place * 2 + my_plane
 
     vals_copy.wait()
-    pair.wait_recv()
-
-    def alpha_step(row, carry):
-        lhs = jnp.concatenate([x_ref[cols_ref[row, k]] for k in range(degree)], axis=1)
-        rhs = jnp.concatenate([vals_v[row, k] for k in range(degree)], axis=1)
-        alpha_ref[row] = lax.dot_general(
-            lhs, rhs, (((1,), (1,)), ((), ())), preferred_element_type=jnp.float32
-        )
-        return carry
-
-    lax.fori_loop(0, half, alpha_step, 0)
 
     @pl.when(active)
     def _():
         pltpu.make_async_copy(y_ref, y_ref, fwd_recv).wait()
 
         def repack(g, carry):
-            for t in range(TILES_PER_PLANE):
+            for t in range(GROUP_TILES):
                 low, high = t * TILE, (t + 1) * TILE
                 pieces = []
                 while low < high:
                     source, begin = low // width, low % width
                     end = min(width, begin + high - low)
-                    piece = y_ref[g * PER_PLANE + source].astype(jnp.float32)
+                    piece = y_ref[g * GROUP_SLICES + source].astype(jnp.float32)
                     pieces.append(piece[begin:end])
                     low += end - begin
-                yt_ref[g * TILES_PER_PLANE + t] = jnp.concatenate(pieces, axis=0).astype(
+                yt_ref[g * GROUP_TILES + t] = jnp.concatenate(pieces, axis=0).astype(
                     jnp.bfloat16
                 )
             return carry
 
-        lax.fori_loop(0, wide // PER_PLANE, repack, 0)
+        lax.fori_loop(0, wide // GROUP_SLICES, repack, 0)
 
         def send_chunk(j):
             send_ref[j] = acc_ref[pl.ds(pl.multiple_of(j * width, 8), width), :].astype(
@@ -161,7 +186,7 @@
                 ).start()
 
         def chunk_of(row):
-            return row + row // TILES_PER_PLANE
+            return row + row // GROUP_TILES
 
         first = lax.rem(w * 7, half)
 
@@ -169,7 +194,7 @@
             row = lax.rem(first + step, half)
             lhs = jnp.concatenate([vals_v[row, k] for k in range(degree)], axis=1)
             rhs = jnp.concatenate(
-                [yt_ref[cols_ref[row, k]] for k in range(degree)],
+                [yt_ref[cols_ref[k, row]] for k in range(degree)],
                 axis=0,
             )
             acc_ref[pl.ds(pl.multiple_of(row * TILE, TILE), TILE), :] = jnp.dot(
@@ -180,7 +205,7 @@
             def _():
                 send_chunk(chunk_of(row))
 
-            @pl.when(lax.rem(row, TILES_PER_PLANE) == TILES_PER_PLANE - 1)
+            @pl.when(lax.rem(row, GROUP_TILES) == GROUP_TILES - 1)
             def _():
                 send_chunk(chunk_of(row) + 1)
 
@@ -188,6 +213,16 @@
 
         lax.fori_loop(0, half, beta_step, 0)
         send_chunk(chunk_of(first))
+
+    def alpha_step(row, carry):
+        lhs = jnp.concatenate([x_ref[cols_ref[k, row]] for k in range(degree)], axis=1)
+        rhs = jnp.concatenate([vals_v[row, k] for k in range(degree)], axis=1)
+        alpha_ref[row] = lax.dot_general(
+            lhs, rhs, (((1,), (1,)), ((), ())), preferred_element_type=jnp.float32
+        )
+        return carry
+
+    lax.fori_loop(0, half, alpha_step, 0)
 
     diag_copy.wait()
     pltpu.make_async_copy(back_ref, back_ref, ret_recv).wait()
@@ -200,20 +235,19 @@
             + diag_v[:, part] * coeff_v[:, part]
         )
 
-    pair.wait_send()
-    has_own = jnp.logical_and(active, tile_half == n)
-
-    @pl.when(has_own)
-    def _():
-        pltpu.make_async_copy(
-            x_ref.at[pl.ds(0, 2 * half - 1)], x_ref.at[pl.ds(0, 2 * half - 1)], fwd_send
-        ).wait()
-
-    @pl.when(jnp.logical_not(has_own))
+    for copy in pair:
+        copy.wait_send()
+
+    @pl.when(active)
+    def _():
+        done = x_ref.at[pl.ds(0, 2 * half - 1)]
+        pltpu.make_async_copy(done, done, fwd_send).wait()
+
+    @pl.when(jnp.logical_not(active))
     def _():
         pltpu.make_async_copy(x_ref, x_ref, fwd_send).wait()
 
-    own_return = jnp.logical_and(has_own, w // half_wide == n)
+    own_return = jnp.logical_and(tile_half == n, w // half_wide == n)
 
     @pl.when(jnp.logical_and(active, own_return))
     def _():
@@ -255,17 +289,17 @@
                 pltpu.VMEM((wide // 2, width, TILE), jnp.bfloat16),
                 pltpu.VMEM((half, width, TILE), jnp.bfloat16),
                 pltpu.SemaphoreType.DMA((3,)),
-                pltpu.SemaphoreType.DMA,
-                pltpu.SemaphoreType.DMA,
+                pltpu.SemaphoreType.DMA((PIECES,)),
+                pltpu.SemaphoreType.DMA((PIECES,)),
                 pltpu.SemaphoreType.DMA,
                 pltpu.SemaphoreType.DMA,
                 pltpu.SemaphoreType.DMA,
                 pltpu.SemaphoreType.DMA,
             ],
             compiler_params=pltpu.CompilerParams(
-                has_side_effects=True, vmem_limit_bytes=52 * 1024 * 1024
+                collective_id=0, has_side_effects=True, vmem_limit_bytes=52 * 1024 * 1024
             ),
-        )(tile_cols, coeffs.T, diagonal.T, tile_vals)
+        )(tile_cols.T, coeffs.T, diagonal.T, tile_vals)
         return out.T
 
     in_specs = (

time: 90.1 us -> 84.4 us (0.937)
  the two profiles are of different devices: /device:TPU:1 before, /device:TPU:45 now
where the time goes in v2:
time: 84.4 us; the launch traced here: 84.2 us
  Pallas kernels  82.3 us (98%)
  local copies, waits for them, and re-layouts  1.94 us (2%)
    pallas_call x1, Pallas kernels, per_device(): pl.pallas_call(functools.partial(kernel, wide=wide, scale=scale), out_sha...  82.3 us
    unnamed x3, local copies, waits for them, and re-layouts  1.94 us

profile of v2, /device:TPU:45, one launch (start us, length us, event | category | flops | bytes accessed | tf_op | source)
XLA Modules:
  0.0 84.2 jit_solution(11236558896366101044)
XLA Ops:
  0.0 0.0 copy-start
  0.0 0.7 copy-done
  0.7 82.3 %shard_map.46 = f32[120,3840]{1,0:T(8,128)S(1)} custom-call(s32[20,30]{1,0:T(8,128)S(1)} %bitcast.5, f32[120,3840]{1,0:T(8,128)} %bitcast.6, f32[120,3840]{1,0:T(8,128)} %bitcast.7, bf16[30,20,128,128]{3,2,1,0:T(8,128)(2,1)} %vals_hbm.1), custom_call_target="tpu_custom_call" | custom-call | tf_op jit(solution)/shard_map/pallas_call | solution.py:270
  83.0 1.2 %copy.6 = f32[3840,120]{0,1:T(8,128)} copy(f32[3840,120]{0,1:T(8,128)S(1)} %bitcast.4) | data formatting | bytes 3686400
Async XLA Ops:
  0.0 0.7 copy-start

commit v3 on v2

--- a/solution.py
+++ b/solution.py
@@ -10,8 +10,7 @@
 
 MESH = pl.DeviceIdType.MESH
 TILE = 128
-PIECES = 5
-PER_SIDE = 16
+PIECES = (9, 8, 6, 4, 2, 1)
 GROUP_SLICES = 16
 GROUP_TILES = 15
 
@@ -78,10 +77,10 @@
 
     pl.semaphore_wait(barrier, 2 * wide - 1)
 
-    piece = half // PIECES
+    starts = [sum(PIECES[:j]) for j in range(len(PIECES))]
     pair = []
-    for j in range(PIECES):
-        part = x_ref.at[pl.ds(n * half + j * piece, piece)]
+    for j, piece in enumerate(PIECES):
+        part = x_ref.at[pl.ds(n * half + starts[j], piece)]
         copy = pltpu.make_async_remote_copy(
             src_ref=part,
             dst_ref=part,
@@ -98,9 +97,7 @@
     def send_forward(tile):
         side, rank = tile // half, lax.rem(tile, half)
         plane = lax.rem(rank, 2)
-        spot = side * (PER_SIDE - 1) + rank // 2
-        spot = spot + spot // (PER_SIDE - 1)
-        to = (spot // 2) * 4 + plane * 2 + lax.rem(spot, 2)
+        to = (rank // 2) * 4 + plane * 2 + side
         to_n = jnp.where(plane == my_plane, n, other)
         mine = jnp.logical_and(to == w, to_n == n)
 
@@ -125,22 +122,31 @@
 
     lax.fori_loop(0, half, send_own, 0)
 
-    for j in range(PIECES):
+    for j, piece in enumerate(PIECES):
         pair[j].wait_recv()
 
         def send_relayed(step, carry):
-            send_forward(other * half + j * piece + lax.rem(w + step, piece))
+            send_forward(other * half + starts[j] + lax.rem(w + step, piece))
             return carry
 
         lax.fori_loop(0, piece, send_relayed, 0)
 
-    my_spot = (w // 4) * 2 + lax.rem(w, 2)
-    tile_half = my_spot // PER_SIDE
-    place = lax.rem(my_spot, PER_SIDE)
-    active = place < PER_SIDE - 1
+    tile_half = lax.rem(w, 2)
+    place = w // 4
+    active = place < half // 2
     slot = place * 2 + my_plane
 
     vals_copy.wait()
+
+    def alpha_step(row, carry):
+        lhs = jnp.concatenate([x_ref[cols_ref[k, row]] for k in range(degree)], axis=1)
+        rhs = jnp.concatenate([vals_v[row, k] for k in range(degree)], axis=1)
+        alpha_ref[row] = lax.dot_general(
+            lhs, rhs, (((1,), (1,)), ((), ())), preferred_element_type=jnp.float32
+        )
+        return carry
+
+    lax.fori_loop(0, half, alpha_step, 0)
 
     @pl.when(active)
     def _():
@@ -213,16 +219,6 @@
 
         lax.fori_loop(0, half, beta_step, 0)
         send_chunk(chunk_of(first))
-
-    def alpha_step(row, carry):
-        lhs = jnp.concatenate([x_ref[cols_ref[k, row]] for k in range(degree)], axis=1)
-        rhs = jnp.concatenate([vals_v[row, k] for k in range(degree)], axis=1)
-        alpha_ref[row] = lax.dot_general(
-            lhs, rhs, (((1,), (1,)), ((), ())), preferred_element_type=jnp.float32
-        )
-        return carry
-
-    lax.fori_loop(0, half, alpha_step, 0)
 
     diag_copy.wait()
     pltpu.make_async_copy(back_ref, back_ref, ret_recv).wait()
@@ -289,8 +285,8 @@
                 pltpu.VMEM((wide // 2, width, TILE), jnp.bfloat16),
                 pltpu.VMEM((half, width, TILE), jnp.bfloat16),
                 pltpu.SemaphoreType.DMA((3,)),
-                pltpu.SemaphoreType.DMA((PIECES,)),
-                pltpu.SemaphoreType.DMA((PIECES,)),
+                pltpu.SemaphoreType.DMA((len(PIECES),)),
+                pltpu.SemaphoreType.DMA((len(PIECES),)),
                 pltpu.SemaphoreType.DMA,
                 pltpu.SemaphoreType.DMA,
                 pltpu.SemaphoreType.DMA,

time: 84.4 us -> 63.6 us (0.75)
  the two profiles are of different devices: /device:TPU:45 before, /device:TPU:1 now
where the time goes in v3:
time: 63.6 us; the launch traced here: 63 us
  Pallas kernels  61.1 us (96%)
  local copies, waits for them, and re-layouts  1.94 us (3%)
    pallas_call x1, Pallas kernels, per_device(): pl.pallas_call(functools.partial(kernel, wide=wide, scale=scale), out_sha...  61.1 us
    unnamed x3, local copies, waits for them, and re-layouts  1.94 us

profile of v3, /device:TPU:1, one launch (start us, length us, event | category | flops | bytes accessed | tf_op | source)
XLA Modules:
  0.0 63.0 jit_solution(8711846876140321107)
XLA Ops:
  0.0 0.0 copy-start
  0.0 0.7 %copy-done = s32[30,20]{0,1:T(8,128)S(1)} copy-done((s32[30,20]{0,1:T(8,128)S(1)}, s32[30,20]{0,1:T(8,128)}, u32[]{:S(2)}) %copy-start) | copy-done | bytes 2424
  0.7 61.1 %shard_map.46 = f32[120,3840]{1,0:T(8,128)S(1)} custom-call(s32[20,30]{1,0:T(8,128)S(1)} %bitcast.5, f32[120,3840]{1,0:T(8,128)} %bitcast.6, f32[120,3840]{1,0:T(8,128)} %bitcast.7, bf16[30,20,128,128]{3,2,1,0:T(8,128)(2,1)} %vals_hbm.1), custom_call_target="tpu_custom_call" | custom-call | tf_op jit(solution)/shard_map/pallas_call | solution.py:266
  61.8 1.2 %copy.6 = f32[3840,120]{0,1:T(8,128)} copy(f32[3840,120]{0,1:T(8,128)S(1)} %bitcast.4) | data formatting | bytes 3686400
Async XLA Ops:
  0.0 0.7 %copy-start = (s32[30,20]{0,1:T(8,128)S(1)}, s32[30,20]{0,1:T(8,128)}, u32[]{:S(2)}) copy-start(s32[30,20]{0,1:T(8,128)} %param.6) | copy-start | bytes 7204

commit v4 on v3

--- a/solution.py
+++ b/solution.py
@@ -10,9 +10,10 @@
 
 MESH = pl.DeviceIdType.MESH
 TILE = 128
-PIECES = (9, 8, 6, 4, 2, 1)
+PIECES = (5, 4, 3, 2, 1)
 GROUP_SLICES = 16
 GROUP_TILES = 15
+ROWS = 5
 
 
 def kernel(
@@ -69,7 +70,7 @@
         pl.semaphore_signal(barrier, inc=1, device_id=(to, other), device_id_type=MESH)
         return carry
 
-    lax.fori_loop(0, wide, greet, 0)
+    lax.fori_loop(0, wide, greet, 0, unroll=8)
     coeff_copy.wait()
 
     for i in range(half):
@@ -77,10 +78,16 @@
 
     pl.semaphore_wait(barrier, 2 * wide - 1)
 
+    my_plane = lax.rem(w // 2, 2)
+    side = lax.rem(my_plane + n, 2)
+    quarter = half // 2
     starts = [sum(PIECES[:j]) for j in range(len(PIECES))]
     pair = []
-    for j, piece in enumerate(PIECES):
-        part = x_ref.at[pl.ds(n * half + starts[j], piece)]
+    for j, piece in enumerate(PIECES + (quarter,)):
+        if j < len(PIECES):
+            part = x_ref.at[pl.ds(n * half + (1 - side) * quarter + starts[j], piece)]
+        else:
+            part = x_ref.at[pl.ds(n * half + side * quarter, quarter)]
         copy = pltpu.make_async_remote_copy(
             src_ref=part,
             dst_ref=part,
@@ -92,14 +99,14 @@
         copy.start()
         pair.append(copy)
 
-    my_plane = lax.rem(w // 2, 2)
-
-    def send_forward(tile):
-        side, rank = tile // half, lax.rem(tile, half)
-        plane = lax.rem(rank, 2)
-        to = (rank // 2) * 4 + plane * 2 + side
-        to_n = jnp.where(plane == my_plane, n, other)
-        mine = jnp.logical_and(to == w, to_n == n)
+    tile_half = lax.rem(w, 2)
+    my_place = w // 4
+    active = my_place < quarter
+    slot = side * quarter + my_place
+
+    def send_forward(from_half, place):
+        tile = from_half * half + side * quarter + place
+        mine = jnp.logical_and(place == my_place, from_half == tile_half)
 
         @pl.when(mine)
         def _():
@@ -112,41 +119,48 @@
                 dst_ref=y_ref.at[w],
                 send_sem=fwd_send,
                 recv_sem=fwd_recv,
-                device_id=(to, to_n),
+                device_id=(place * 4 + my_plane * 2 + from_half, n),
                 device_id_type=MESH,
             ).start()
 
+        pltpu.make_async_remote_copy(
+            src_ref=x_ref.at[tile],
+            dst_ref=y_ref.at[w],
+            send_sem=fwd_send,
+            recv_sem=fwd_recv,
+            device_id=(place * 4 + (1 - my_plane) * 2 + from_half, other),
+            device_id_type=MESH,
+        ).start()
+
     def send_own(step, carry):
-        send_forward(n * half + lax.rem(w * 7 + step, half))
+        send_forward(n, lax.rem(w * 7 + step, quarter))
         return carry
 
-    lax.fori_loop(0, half, send_own, 0)
+    lax.fori_loop(0, quarter, send_own, 0)
 
     for j, piece in enumerate(PIECES):
         pair[j].wait_recv()
 
         def send_relayed(step, carry):
-            send_forward(other * half + starts[j] + lax.rem(w + step, piece))
+            send_forward(other, starts[j] + lax.rem(w + step, piece))
             return carry
 
         lax.fori_loop(0, piece, send_relayed, 0)
 
-    tile_half = lax.rem(w, 2)
-    place = w // 4
-    active = place < half // 2
-    slot = place * 2 + my_plane
-
     vals_copy.wait()
-
-    def alpha_step(row, carry):
-        lhs = jnp.concatenate([x_ref[cols_ref[k, row]] for k in range(degree)], axis=1)
-        rhs = jnp.concatenate([vals_v[row, k] for k in range(degree)], axis=1)
-        alpha_ref[row] = lax.dot_general(
-            lhs, rhs, (((1,), (1,)), ((), ())), preferred_element_type=jnp.float32
-        )
+    pair[-1].wait_recv()
+
+    def alpha_group(group, carry):
+        for u in range(ROWS):
+            row = group * ROWS + u
+            lhs = jnp.concatenate([x_ref[cols_ref[k, row]] for k in range(degree)], axis=1)
+            rhs = jnp.concatenate([vals_v[row, k] for k in range(degree)], axis=1)
+            alpha_ref[row] = lax.dot_general(
+                lhs, rhs, (((1,), (1,)), ((), ())), preferred_element_type=jnp.float32
+            )
         return carry
 
-    lax.fori_loop(0, half, alpha_step, 0)
+    lax.fori_loop(0, half // ROWS, alpha_group, 0)
 
     @pl.when(active)
     def _():
@@ -191,34 +205,38 @@
                     device_id_type=MESH,
                 ).start()
 
-        def chunk_of(row):
-            return row + row // GROUP_TILES
-
-        first = lax.rem(w * 7, half)
-
-        def beta_step(step, carry):
-            row = lax.rem(first + step, half)
-            lhs = jnp.concatenate([vals_v[row, k] for k in range(degree)], axis=1)
-            rhs = jnp.concatenate(
-                [yt_ref[cols_ref[k, row]] for k in range(degree)],
-                axis=0,
-            )
-            acc_ref[pl.ds(pl.multiple_of(row * TILE, TILE), TILE), :] = jnp.dot(
-                lhs, rhs, preferred_element_type=jnp.float32
-            )
-
-            @pl.when(step > 0)
+        groups = half // ROWS
+        per_block = GROUP_TILES // ROWS
+        first = lax.rem(w + w // 16, groups)
+
+        def beta_group(step, carry):
+            group = lax.rem(first + step, groups)
+            for u in range(ROWS):
+                row = group * ROWS + u
+                lhs = jnp.concatenate([vals_v[row, k] for k in range(degree)], axis=1)
+                rhs = jnp.concatenate([yt_ref[cols_ref[k, row]] for k in range(degree)], axis=0)
+                acc_ref[pl.ds(pl.multiple_of(row * TILE, TILE), TILE), :] = jnp.dot(
+                    lhs, rhs, preferred_element_type=jnp.float32
+                )
+            chunk = group * ROWS + group // per_block
+            spot = lax.rem(group, per_block)
+
+            @pl.when(jnp.logical_or(step > 0, spot == 0))
             def _():
-                send_chunk(chunk_of(row))
-
-            @pl.when(lax.rem(row, GROUP_TILES) == GROUP_TILES - 1)
-            def _():
-                send_chunk(chunk_of(row) + 1)
-
+                send_chunk(chunk)
+
+            def send_rest(u, carry):
+                send_chunk(chunk + u)
+                return carry
+
+            lax.fori_loop(1, jnp.where(spot == per_block - 1, ROWS + 1, ROWS), send_rest, 0)
             return carry
 
-        lax.fori_loop(0, half, beta_step, 0)
-        send_chunk(chunk_of(first))
+        lax.fori_loop(0, groups, beta_group, 0)
+
+        @pl.when(lax.rem(first, per_block) != 0)
+        def _():
+            send_chunk(first * ROWS + first // per_block)
 
     diag_copy.wait()
     pltpu.make_async_copy(back_ref, back_ref, ret_recv).wait()
@@ -285,8 +303,8 @@
                 pltpu.VMEM((wide // 2, width, TILE), jnp.bfloat16),
                 pltpu.VMEM((half, width, TILE), jnp.bfloat16),
                 pltpu.SemaphoreType.DMA((3,)),
-                pltpu.SemaphoreType.DMA((len(PIECES),)),
-                pltpu.SemaphoreType.DMA((len(PIECES),)),
+                pltpu.SemaphoreType.DMA((len(PIECES) + 1,)),
+                pltpu.SemaphoreType.DMA((len(PIECES) + 1,)),
                 pltpu.SemaphoreType.DMA,
                 pltpu.SemaphoreType.DMA,
                 pltpu.SemaphoreType.DMA,

time: 63.6 us -> 57.9 us (0.910)
  Pallas kernels: 61.1 us -> 55.8 us
    pallas_call x1, Pallas kernels: 61.1 us -> 55.8 us  [per_device(): pl.pallas_call(functools.partial(kernel, wide=wide, scale=scale), out_sha...]
where the time goes in v4:
time: 57.9 us; the launch traced here: 57.7 us
  Pallas kernels  55.8 us (96%)
  local copies, waits for them, and re-layouts  1.94 us (3%)
    pallas_call x1, Pallas kernels, per_device(): pl.pallas_call(functools.partial(kernel, wide=wide, scale=scale), out_sha...  55.8 us
    unnamed x3, local copies, waits for them, and re-layouts  1.94 us

profile of v4, /device:TPU:1, one launch (start us, length us, event | category | flops | bytes accessed | tf_op | source)
XLA Modules:
  0.0 57.7 jit_solution(5507397425413799321)
XLA Ops:
  0.0 0.0 copy-start
  0.0 0.7 %copy-done = s32[30,20]{0,1:T(8,128)S(1)} copy-done((s32[30,20]{0,1:T(8,128)S(1)}, s32[30,20]{0,1:T(8,128)}, u32[]{:S(2)}) %copy-start) | copy-done | bytes 2424
  0.7 55.8 %shard_map.46 = f32[120,3840]{1,0:T(8,128)S(1)} custom-call(s32[20,30]{1,0:T(8,128)S(1)} %bitcast.5, f32[120,3840]{1,0:T(8,128)} %bitcast.6, f32[120,3840]{1,0:T(8,128)} %bitcast.7, bf16[30,20,128,128]{3,2,1,0:T(8,128)(2,1)} %vals_hbm.1), custom_call_target="tpu_custom_call" | custom-call | tf_op jit(solution)/shard_map/pallas_call | solution.py:284
  56.5 1.2 %copy.6 = f32[3840,120]{0,1:T(8,128)} copy(f32[3840,120]{0,1:T(8,128)S(1)} %bitcast.4) | data formatting | bytes 3686400
Async XLA Ops:
  0.0 0.7 %copy-start = (s32[30,20]{0,1:T(8,128)S(1)}, s32[30,20]{0,1:T(8,128)}, u32[]{:S(2)}) copy-start(s32[30,20]{0,1:T(8,128)} %param.6) | copy-start | bytes 7204

commit v5 on v4

--- a/solution.py
+++ b/solution.py
@@ -17,11 +17,12 @@
 
 
 def kernel(
-    cols_ref,
+    cols_hbm,
     coeff_hbm,
     diag_hbm,
     vals_hbm,
     out_ref,
+    cols_ref,
     coeff_v,
     diag_v,
     vals_v,
@@ -57,6 +58,8 @@
     vals_copy.start()
     diag_copy = pltpu.make_async_copy(diag_hbm, diag_v, local_sem.at[2])
     diag_copy.start()
+    cols_copy = pltpu.make_async_copy(cols_hbm, cols_ref, local_sem.at[3])
+    cols_copy.start()
 
     barrier = pltpu.get_barrier_semaphore()
 
@@ -99,7 +102,7 @@
         copy.start()
         pair.append(copy)
 
-    tile_half = lax.rem(w, 2)
+    tile_half = lax.rem(w + my_plane, 2)
     my_place = w // 4
     active = my_place < quarter
     slot = side * quarter + my_place
@@ -119,7 +122,7 @@
                 dst_ref=y_ref.at[w],
                 send_sem=fwd_send,
                 recv_sem=fwd_recv,
-                device_id=(place * 4 + my_plane * 2 + from_half, n),
+                device_id=(place * 4 + my_plane * 2 + lax.rem(from_half + my_plane, 2), n),
                 device_id_type=MESH,
             ).start()
 
@@ -128,7 +131,10 @@
             dst_ref=y_ref.at[w],
             send_sem=fwd_send,
             recv_sem=fwd_recv,
-            device_id=(place * 4 + (1 - my_plane) * 2 + from_half, other),
+            device_id=(
+                place * 4 + (1 - my_plane) * 2 + lax.rem(from_half + 1 - my_plane, 2),
+                other,
+            ),
             device_id_type=MESH,
         ).start()
 
@@ -148,19 +154,7 @@
         lax.fori_loop(0, piece, send_relayed, 0)
 
     vals_copy.wait()
-    pair[-1].wait_recv()
-
-    def alpha_group(group, carry):
-        for u in range(ROWS):
-            row = group * ROWS + u
-            lhs = jnp.concatenate([x_ref[cols_ref[k, row]] for k in range(degree)], axis=1)
-            rhs = jnp.concatenate([vals_v[row, k] for k in range(degree)], axis=1)
-            alpha_ref[row] = lax.dot_general(
-                lhs, rhs, (((1,), (1,)), ((), ())), preferred_element_type=jnp.float32
-            )
-        return carry
-
-    lax.fori_loop(0, half // ROWS, alpha_group, 0)
+    cols_copy.wait()
 
     @pl.when(active)
     def _():
@@ -238,16 +232,29 @@
         def _():
             send_chunk(first * ROWS + first // per_block)
 
+    pair[-1].wait_recv()
+
+    def alpha_group(group, carry):
+        for u in range(ROWS):
+            row = group * ROWS + u
+            lhs = jnp.concatenate([x_ref[cols_ref[k, row]] for k in range(degree)], axis=1)
+            rhs = jnp.concatenate([vals_v[row, k] for k in range(degree)], axis=1)
+            alpha_ref[row] = lax.dot_general(
+                lhs, rhs, (((1,), (1,)), ((), ())), preferred_element_type=jnp.float32
+            )
+        return carry
+
+    lax.fori_loop(0, half // ROWS, alpha_group, 0)
+
     diag_copy.wait()
-    pltpu.make_async_copy(back_ref, back_ref, ret_recv).wait()
-
     for i in range(half):
         part = slice(i * TILE, (i + 1) * TILE)
-        out_ref[:, part] = (
-            scale * alpha_ref[i]
-            + scale * back_ref[i].astype(jnp.float32)
-            + diag_v[:, part] * coeff_v[:, part]
-        )
+        out_ref[:, part] = scale * alpha_ref[i] + diag_v[:, part] * coeff_v[:, part]
+
+    pltpu.make_async_copy(back_ref, back_ref, ret_recv).wait()
+    for i in range(half):
+        part = slice(i * TILE, (i + 1) * TILE)
+        out_ref[:, part] += scale * back_ref[i].astype(jnp.float32)
 
     for copy in pair:
         copy.wait_send()
@@ -285,13 +292,14 @@
             functools.partial(kernel, wide=wide, scale=scale),
             out_shape=jax.ShapeDtypeStruct((width, rows), jnp.float32),
             in_specs=[
-                pl.BlockSpec(memory_space=pltpu.SMEM),
+                any_space,
                 any_space,
                 any_space,
                 any_space,
             ],
             out_specs=pl.BlockSpec(memory_space=pltpu.VMEM),
             scratch_shapes=[
+                pltpu.SMEM((degree, half), jnp.int32),
                 pltpu.VMEM((width, rows), jnp.float32),
                 pltpu.VMEM((width, rows), jnp.float32),
                 pltpu.VMEM((half, degree, TILE, TILE), jnp.bfloat16),
@@ -302,7 +310,7 @@
                 pltpu.VMEM((half, width, TILE), jnp.float32),
                 pltpu.VMEM((wide // 2, width, TILE), jnp.bfloat16),
                 pltpu.VMEM((half, width, TILE), jnp.bfloat16),
-                pltpu.SemaphoreType.DMA((3,)),
+                pltpu.SemaphoreType.DMA((4,)),
                 pltpu.SemaphoreType.DMA((len(PIECES) + 1,)),
                 pltpu.SemaphoreType.DMA((len(PIECES) + 1,)),
                 pltpu.SemaphoreType.DMA,

time: 57.9 us -> 55.8 us (0.964)
  Pallas kernels: 55.8 us -> 53.7 us
    pallas_call x1, Pallas kernels: 55.8 us -> 53.7 us  [per_device(): pl.pallas_call(functools.partial(kernel, wide=wide, scale=scale), out_sha...]
where the time goes in v5:
time: 55.8 us; the launch traced here: 55.6 us
  Pallas kernels  53.7 us (96%)
  local copies, waits for them, and re-layouts  1.94 us (3%)
    pallas_call x1, Pallas kernels, per_device(): pl.pallas_call(functools.partial(kernel, wide=wide, scale=scale), out_sha...  53.7 us
    unnamed x3, local copies, waits for them, and re-layouts  1.94 us

profile of v5, /device:TPU:1, one launch (start us, length us, event | category | flops | bytes accessed | tf_op | source)
XLA Modules:
  0.0 55.6 jit_solution(1160184090171743837)
XLA Ops:
  0.0 0.0 copy-start
  0.0 0.7 %copy-done = s32[30,20]{0,1:T(8,128)S(1)} copy-done((s32[30,20]{0,1:T(8,128)S(1)}, s32[30,20]{0,1:T(8,128)}, u32[]{:S(2)}) %copy-start) | copy-done | bytes 2424
  0.7 53.7 %shard_map.46 = f32[120,3840]{1,0:T(8,128)S(1)} custom-call(s32[20,30]{1,0:T(8,128)S(1)} %bitcast.5, f32[120,3840]{1,0:T(8,128)} %bitcast.6, f32[120,3840]{1,0:T(8,128)} %bitcast.7, bf16[30,20,128,128]{3,2,1,0:T(8,128)(2,1)} %vals_hbm.1), custom_call_target="tpu_custom_call" | custom-call | tf_op jit(solution)/shard_map/pallas_call | solution.py:291
  54.4 1.2 %copy.6 = f32[3840,120]{0,1:T(8,128)} copy(f32[3840,120]{0,1:T(8,128)S(1)} %bitcast.4) | data formatting | bytes 3686400
Async XLA Ops:
  0.0 0.7 %copy-start = (s32[30,20]{0,1:T(8,128)S(1)}, s32[30,20]{0,1:T(8,128)}, u32[]{:S(2)}) copy-start(s32[30,20]{0,1:T(8,128)} %param.6) | copy-start | bytes 7204

commit v6 on v5

--- a/solution.py
+++ b/solution.py
@@ -54,27 +54,27 @@
 
     coeff_copy = pltpu.make_async_copy(coeff_hbm, coeff_v, local_sem.at[0])
     coeff_copy.start()
+
+    barrier = pltpu.get_barrier_semaphore()
+
+    def greet(step, carry):
+        to = lax.rem(w + step, wide)
+
+        @pl.when(step > 0)
+        def _():
+            pl.semaphore_signal(barrier, inc=1, device_id=(to, n), device_id_type=MESH)
+
+        pl.semaphore_signal(barrier, inc=1, device_id=(to, other), device_id_type=MESH)
+        return carry
+
+    lax.fori_loop(0, wide, greet, 0, unroll=8)
+    coeff_copy.wait()
     vals_copy = pltpu.make_async_copy(vals_hbm, vals_v, local_sem.at[1])
     vals_copy.start()
     diag_copy = pltpu.make_async_copy(diag_hbm, diag_v, local_sem.at[2])
     diag_copy.start()
     cols_copy = pltpu.make_async_copy(cols_hbm, cols_ref, local_sem.at[3])
     cols_copy.start()
-
-    barrier = pltpu.get_barrier_semaphore()
-
-    def greet(step, carry):
-        to = lax.rem(w + step, wide)
-
-        @pl.when(step > 0)
-        def _():
-            pl.semaphore_signal(barrier, inc=1, device_id=(to, n), device_id_type=MESH)
-
-        pl.semaphore_signal(barrier, inc=1, device_id=(to, other), device_id_type=MESH)
-        return carry
-
-    lax.fori_loop(0, wide, greet, 0, unroll=8)
-    coeff_copy.wait()
 
     for i in range(half):
         x_ref[n * half + i] = coeff_v[:, i * TILE : (i + 1) * TILE].astype(jnp.bfloat16)
@@ -99,7 +99,8 @@
             device_id=(w, other),
             device_id_type=MESH,
         )
-        copy.start()
+        if j < len(PIECES):
+            copy.start()
         pair.append(copy)
 
     tile_half = lax.rem(w + my_plane, 2)
@@ -152,6 +153,8 @@
             return carry
 
         lax.fori_loop(0, piece, send_relayed, 0)
+
+    pair[-1].start()
 
     vals_copy.wait()
     cols_copy.wait()
@@ -201,7 +204,9 @@
 
         groups = half // ROWS
         per_block = GROUP_TILES // ROWS
-        first = lax.rem(w + w // 16, groups)
+        number = lax.rem(my_place * 7 + my_plane * 15, half)
+        first = lax.rem(number, groups)
+        turn = number // groups
 
         def beta_group(step, carry):
             group = lax.rem(first + step, groups)
@@ -215,15 +220,21 @@
             chunk = group * ROWS + group // per_block
             spot = lax.rem(group, per_block)
 
-            @pl.when(jnp.logical_or(step > 0, spot == 0))
+            def send_one(i, carry):
+                u = lax.rem(turn + i, ROWS)
+
+                @pl.when(jnp.logical_or(step + u > 0, spot == 0))
+                def _():
+                    send_chunk(chunk + u)
+
+                return carry
+
+            lax.fori_loop(0, ROWS, send_one, 0)
+
+            @pl.when(spot == per_block - 1)
             def _():
-                send_chunk(chunk)
-
-            def send_rest(u, carry):
-                send_chunk(chunk + u)
-                return carry
-
-            lax.fori_loop(1, jnp.where(spot == per_block - 1, ROWS + 1, ROWS), send_rest, 0)
+                send_chunk(chunk + ROWS)
+
             return carry
 
         lax.fori_loop(0, groups, beta_group, 0)

time: 55.8 us -> 55.8 us (level)
  no operation moved by 1% of the time
where the time goes in v6:
time: 55.8 us; the launch traced here: 55.6 us
  Pallas kernels  53.7 us (96%)
  local copies, waits for them, and re-layouts  1.94 us (3%)
    pallas_call x1, Pallas kernels, per_device(): pl.pallas_call(functools.partial(kernel, wide=wide, scale=scale), out_sha...  53.7 us
    unnamed x3, local copies, waits for them, and re-layouts  1.94 us

profile of v6, /device:TPU:1, one launch (start us, length us, event | category | flops | bytes accessed | tf_op | source)
XLA Modules:
  0.0 55.6 jit_solution(16435964712289314711)
XLA Ops:
  0.0 0.0 copy-start
  0.0 0.7 %copy-done = s32[30,20]{0,1:T(8,128)S(1)} copy-done((s32[30,20]{0,1:T(8,128)S(1)}, s32[30,20]{0,1:T(8,128)}, u32[]{:S(2)}) %copy-start) | copy-done | bytes 2424
  0.7 53.7 %shard_map.46 = f32[120,3840]{1,0:T(8,128)S(1)} custom-call(s32[20,30]{1,0:T(8,128)S(1)} %bitcast.5, f32[120,3840]{1,0:T(8,128)} %bitcast.6, f32[120,3840]{1,0:T(8,128)} %bitcast.7, bf16[30,20,128,128]{3,2,1,0:T(8,128)(2,1)} %vals_hbm.1), custom_call_target="tpu_custom_call" | custom-call | tf_op jit(solution)/shard_map/pallas_call | solution.py:302
  54.4 1.2 %copy.6 = f32[3840,120]{0,1:T(8,128)} copy(f32[3840,120]{0,1:T(8,128)S(1)} %bitcast.4) | data formatting | bytes 3686400
Async XLA Ops:
  0.0 0.7 %copy-start = (s32[30,20]{0,1:T(8,128)S(1)}, s32[30,20]{0,1:T(8,128)}, u32[]{:S(2)}) copy-start(s32[30,20]{0,1:T(8,128)} %param.6) | copy-start | bytes 7204

commit v7 on v5

--- a/solution.py
+++ b/solution.py
@@ -102,8 +102,8 @@
         copy.start()
         pair.append(copy)
 
-    tile_half = lax.rem(w + my_plane, 2)
     my_place = w // 4
+    tile_half = lax.rem(w + my_plane + my_place, 2)
     active = my_place < quarter
     slot = side * quarter + my_place
 
@@ -122,7 +122,7 @@
                 dst_ref=y_ref.at[w],
                 send_sem=fwd_send,
                 recv_sem=fwd_recv,
-                device_id=(place * 4 + my_plane * 2 + lax.rem(from_half + my_plane, 2), n),
+                device_id=(place * 4 + my_plane * 2 + lax.rem(from_half + my_plane + place, 2), n),
                 device_id_type=MESH,
             ).start()
 
@@ -132,7 +132,7 @@
             send_sem=fwd_send,
             recv_sem=fwd_recv,
             device_id=(
-                place * 4 + (1 - my_plane) * 2 + lax.rem(from_half + 1 - my_plane, 2),
+                place * 4 + (1 - my_plane) * 2 + lax.rem(from_half + 1 - my_plane + place, 2),
                 other,
             ),
             device_id_type=MESH,

time: 55.8 us -> 55.7 us (level)
  no operation moved by 1% of the time
where the time goes in v7:
time: 55.7 us; the launch traced here: 55.6 us
  Pallas kernels  53.6 us (96%)
  local copies, waits for them, and re-layouts  1.94 us (3%)
    pallas_call x1, Pallas kernels, per_device(): pl.pallas_call(functools.partial(kernel, wide=wide, scale=scale), out_sha...  53.6 us
    unnamed x3, local copies, waits for them, and re-layouts  1.94 us

profile of v7, /device:TPU:1, one launch (start us, length us, event | category | flops | bytes accessed | tf_op | source)
XLA Modules:
  0.0 55.6 jit_solution(9581143246080000751)
XLA Ops:
  0.0 0.0 copy-start
  0.0 0.7 %copy-done = s32[30,20]{0,1:T(8,128)S(1)} copy-done((s32[30,20]{0,1:T(8,128)S(1)}, s32[30,20]{0,1:T(8,128)}, u32[]{:S(2)}) %copy-start) | copy-done | bytes 2424
  0.7 53.6 %shard_map.46 = f32[120,3840]{1,0:T(8,128)S(1)} custom-call(s32[20,30]{1,0:T(8,128)S(1)} %bitcast.5, f32[120,3840]{1,0:T(8,128)} %bitcast.6, f32[120,3840]{1,0:T(8,128)} %bitcast.7, bf16[30,20,128,128]{3,2,1,0:T(8,128)(2,1)} %vals_hbm.1), custom_call_target="tpu_custom_call" | custom-call | tf_op jit(solution)/shard_map/pallas_call | solution.py:291
  54.3 1.2 %copy.6 = f32[3840,120]{0,1:T(8,128)} copy(f32[3840,120]{0,1:T(8,128)S(1)} %bitcast.4) | data formatting | bytes 3686400
Async XLA Ops:
  0.0 0.7 %copy-start = (s32[30,20]{0,1:T(8,128)S(1)}, s32[30,20]{0,1:T(8,128)}, u32[]{:S(2)}) copy-start(s32[30,20]{0,1:T(8,128)} %param.6) | copy-start | bytes 7204

commit v8 on v7

--- a/solution.py
+++ b/solution.py
@@ -99,7 +99,8 @@
             device_id=(w, other),
             device_id_type=MESH,
         )
-        copy.start()
+        if j < len(PIECES):
+            copy.start()
         pair.append(copy)
 
     my_place = w // 4
@@ -152,6 +153,8 @@
             return carry
 
         lax.fori_loop(0, piece, send_relayed, 0)
+
+    pair[-1].start()
 
     vals_copy.wait()
     cols_copy.wait()

time: 55.7 us -> 55.7 us (level)
  no operation moved by 1% of the time
where the time goes in v8:
time: 55.7 us; the launch traced here: 55.6 us
  Pallas kernels  53.6 us (96%)
  local copies, waits for them, and re-layouts  1.94 us (3%)
    pallas_call x1, Pallas kernels, per_device(): pl.pallas_call(functools.partial(kernel, wide=wide, scale=scale), out_sha...  53.6 us
    unnamed x3, local copies, waits for them, and re-layouts  1.94 us

profile of v8, /device:TPU:1, one launch (start us, length us, event | category | flops | bytes accessed | tf_op | source)
XLA Modules:
  0.0 55.6 jit_solution(2361065604426660219)
XLA Ops:
  0.0 0.0 copy-start
  0.0 0.7 %copy-done = s32[30,20]{0,1:T(8,128)S(1)} copy-done((s32[30,20]{0,1:T(8,128)S(1)}, s32[30,20]{0,1:T(8,128)}, u32[]{:S(2)}) %copy-start) | copy-done | bytes 2424
  0.7 53.6 %shard_map.46 = f32[120,3840]{1,0:T(8,128)S(1)} custom-call(s32[20,30]{1,0:T(8,128)S(1)} %bitcast.5, f32[120,3840]{1,0:T(8,128)} %bitcast.6, f32[120,3840]{1,0:T(8,128)} %bitcast.7, bf16[30,20,128,128]{3,2,1,0:T(8,128)(2,1)} %vals_hbm.1), custom_call_target="tpu_custom_call" | custom-call | tf_op jit(solution)/shard_map/pallas_call | solution.py:294
  54.3 1.2 %copy.6 = f32[3840,120]{0,1:T(8,128)} copy(f32[3840,120]{0,1:T(8,128)S(1)} %bitcast.4) | data formatting | bytes 3686400
Async XLA Ops:
  0.0 0.7 %copy-start = (s32[30,20]{0,1:T(8,128)S(1)}, s32[30,20]{0,1:T(8,128)}, u32[]{:S(2)}) copy-start(s32[30,20]{0,1:T(8,128)} %param.6) | copy-start | bytes 7204

commit v9 on v8

--- a/solution.py
+++ b/solution.py
@@ -73,7 +73,7 @@
         pl.semaphore_signal(barrier, inc=1, device_id=(to, other), device_id_type=MESH)
         return carry
 
-    lax.fori_loop(0, wide, greet, 0, unroll=8)
+    lax.fori_loop(0, wide, greet, 0, unroll=32)
     coeff_copy.wait()
 
     for i in range(half):

time: 55.7 us -> 55.7 us (level)
  no operation moved by 1% of the time
where the time goes in v9:
time: 55.7 us; the launch traced here: 55.6 us
  Pallas kernels  53.6 us (96%)
  local copies, waits for them, and re-layouts  1.94 us (3%)
    pallas_call x1, Pallas kernels, per_device(): pl.pallas_call(functools.partial(kernel, wide=wide, scale=scale), out_sha...  53.6 us
    unnamed x3, local copies, waits for them, and re-layouts  1.94 us

profile of v9, /device:TPU:1, one launch (start us, length us, event | category | flops | bytes accessed | tf_op | source)
XLA Modules:
  0.0 55.6 jit_solution(6574191284696241909)
XLA Ops:
  0.0 0.0 copy-start
  0.0 0.7 %copy-done = s32[30,20]{0,1:T(8,128)S(1)} copy-done((s32[30,20]{0,1:T(8,128)S(1)}, s32[30,20]{0,1:T(8,128)}, u32[]{:S(2)}) %copy-start) | copy-done | bytes 2424
  0.7 53.6 %shard_map.46 = f32[120,3840]{1,0:T(8,128)S(1)} custom-call(s32[20,30]{1,0:T(8,128)S(1)} %bitcast.5, f32[120,3840]{1,0:T(8,128)} %bitcast.6, f32[120,3840]{1,0:T(8,128)} %bitcast.7, bf16[30,20,128,128]{3,2,1,0:T(8,128)(2,1)} %vals_hbm.1), custom_call_target="tpu_custom_call" | custom-call | tf_op jit(solution)/shard_map/pallas_call | solution.py:294
  54.3 1.2 %copy.6 = f32[3840,120]{0,1:T(8,128)} copy(f32[3840,120]{0,1:T(8,128)S(1)} %bitcast.4) | data formatting | bytes 3686400
Async XLA Ops:
  0.0 0.7 %copy-start = (s32[30,20]{0,1:T(8,128)S(1)}, s32[30,20]{0,1:T(8,128)}, u32[]{:S(2)}) copy-start(s32[30,20]{0,1:T(8,128)} %param.6) | copy-start | bytes 7204
